TPU v7x, 32 devices: a whole 2x2x4 slice. The times are simulated.
32 devices in a mesh: sub: 8 (over z, y), grp: 4 (over x, core).
Axes of the slice: x: 2, y: 2, z: 4, core: 2. Of those that a mesh axis runs over, the one named last changes fastest.
Arguments:
- right_side: float32 [512, 8192], P('grp', 'sub'), may hold values from -6 to 6
- operator_block: bfloat16 [8192, 1024], P('sub'), may hold values from -0.1875 to 0.1875
- operator_diag: float32 [8192], P('sub'), may hold values from 2 to 4
- solve_block: bfloat16 [8192, 1024], P('sub'), may hold values from -0.1875 to 0.1875
- solve_diag: float32 [8192], P('sub'), may hold values from 0.5 to 1.5
- upper_rows: int32 [8, 128], P('sub'), may hold values from 0 to 1023, as said below
- lower_rows: int32 [8, 128], P('sub'), may hold values from 0 to 1023, as said below
- couple_up: bfloat16 [1024, 128], P('sub'), may hold values from -0.5 to 0.5
- couple_down: bfloat16 [1024, 128], P('sub'), may hold values from -0.5 to 0.5
- coarse_basis: bfloat16 [64, 8192], P(None, 'sub'), may hold values from -0.75 to 0.75
- coarse_inverse: bfloat16 [512, 512], P(('sub', 'grp')), may hold values from -0.046875 to 0.046875
Outputs:
- solution: float32 [512, 8192], P('grp', 'sub')
Inputs may be any that keep to these rules, and one draw needn't show every extreme that they name: `upper_rows`: local row numbers within a subdomain of 1024 unknowns; the 128 entries of one subdomain are distinct, and none of them appears in lower_rows of the same subdomain. `lower_rows`: local row numbers within a subdomain of 1024 unknowns; the 128 entries of one subdomain are distinct, and none of them appears in upper_rows of the same subdomain.
All inputs are finite; a program needn't handle non-finite values.
Results may differ from a plain program's by a relative error of at most 0.0042.
Values may be sent and summed in bfloat16 or wider, within the bound.
A program may use at most 64 MiB of HBM per device.

v0:
```python
import jax
import jax.numpy as jnp
from jax import lax
from jax.sharding import PartitionSpec as P

ITERS = 3
EPS = 1e-06


def extended(block, sides, width):
    for axis, dim in sides:
        count = lax.axis_size(axis)
        forward = [(i, i + 1) for i in range(count - 1)]
        forward.append((count - 1, 0))
        backward = [(target, source) for source, target in forward]
        low = lax.ppermute(
            lax.slice_in_dim(block, block.shape[dim] - width, None, axis=dim), axis, forward
        )
        high = lax.ppermute(lax.slice_in_dim(block, 0, width, axis=dim), axis, backward)
        block = jnp.concatenate([low, block, high], axis=dim)
    return block


def contract_last(left, right):
    return lax.dot_general(
        left, right, (((1,), (1,)), ((), ())), preferred_element_type=jnp.float32
    )


def apply_operator(
    vector, operator_block, operator_diag, upper_list, lower_list, couple_up, couple_down
):
    vector_b = vector.astype(jnp.bfloat16)
    product = contract_last(vector_b, operator_block)
    face_count = upper_list.shape[0]
    upper_face = jnp.take(vector_b, upper_list, axis=1)
    lower_face = jnp.take(vector_b, lower_list, axis=1)
    two_faces = jnp.concatenate([lower_face, upper_face], axis=1)
    padded = extended(two_faces, (("sub", 1),), face_count)
    from_below = padded[:, :face_count]
    from_above = padded[:, 3 * face_count :]
    into_upper = jnp.dot(from_above, couple_up, preferred_element_type=jnp.float32)
    into_lower = jnp.dot(from_below, couple_down, preferred_element_type=jnp.float32)
    result = operator_diag[None, :] * vector + product
    result = result.at[:, upper_list].add(into_upper)
    result = result.at[:, lower_list].add(into_lower)
    return result


def apply_solve(vector, solve_block, solve_diag, coarse_basis, coarse_inverse):
    vector_b = vector.astype(jnp.bfloat16)
    local_term = contract_last(vector_b, solve_block)
    partial_res = contract_last(coarse_basis, vector_b).astype(jnp.bfloat16)
    widened = lax.all_gather(partial_res, "grp", axis=1, tiled=True)
    solved_part = jnp.dot(
        coarse_inverse,
        lax.all_gather(widened, "sub", axis=0, tiled=True),
        preferred_element_type=jnp.float32,
    ).astype(jnp.bfloat16)
    solved = lax.all_to_all(solved_part, "grp", split_axis=1, concat_axis=0, tiled=True)
    coarse_term = lax.dot_general(
        solved, coarse_basis, (((0,), (0,)), ((), ())), preferred_element_type=jnp.float32
    )
    return solve_diag[None, :] * vector + local_term + coarse_term


def norm_of(vector):
    squares = jnp.sum(vector * vector, axis=1)
    return jnp.sqrt(lax.psum(squares, "sub") + EPS)


def least_squares(initial_norm, columns):
    extent = len(columns)
    rotations = []
    target = [initial_norm] + [jnp.zeros_like(initial_norm) for _ in range(extent)]
    triangle = []
    for j in range(extent):
        column = list(columns[j])
        for i in range(j):
            cosine, sine_value = rotations[i]
            leading = cosine * column[i] + sine_value * column[i + 1]
            column[i + 1] = -sine_value * column[i] + cosine * column[i + 1]
            column[i] = leading
        radius = jnp.sqrt(column[j] * column[j] + column[j + 1] * column[j + 1])
        cosine = column[j] / radius
        sine_value = column[j + 1] / radius
        column[j] = radius
        rotations.append((cosine, sine_value))
        target[j + 1] = -sine_value * target[j]
        target[j] = cosine * target[j]
        triangle.append(column[: j + 1])
    coeffs = [None] * extent
    for j in reversed(range(extent)):
        partial_sum = target[j]
        for k in range(j + 1, extent):
            partial_sum = partial_sum - triangle[k][j] * coeffs[k]
        coeffs[j] = partial_sum / triangle[j][j]
    return coeffs


def on_device(
    right_side,
    operator_block,
    operator_diag,
    solve_block,
    solve_diag,
    upper_rows,
    lower_rows,
    couple_up,
    couple_down,
    coarse_basis,
    coarse_inverse,
):
    upper_list = upper_rows.reshape(-1)
    lower_list = lower_rows.reshape(-1)

    def precond(vector):
        return apply_solve(vector, solve_block, solve_diag, coarse_basis, coarse_inverse)

    residual = precond(right_side)
    initial_norm = norm_of(residual)
    krylov = [residual / initial_norm[:, None]]
    columns = []
    for iteration in range(ITERS):
        candidate = precond(
            apply_operator(
                krylov[iteration],
                operator_block,
                operator_diag,
                upper_list,
                lower_list,
                couple_up,
                couple_down,
            )
        )
        heights = []
        for i in range(iteration + 1):
            height_i = lax.psum(jnp.sum(candidate * krylov[i], axis=1), "sub")
            heights.append(height_i)
            candidate = candidate - height_i[:, None] * krylov[i]
        height = norm_of(candidate)
        heights.append(height)
        krylov.append(candidate / height[:, None])
        columns.append(heights)
    coeffs = least_squares(initial_norm, columns)
    solution = coeffs[0][:, None] * krylov[0]
    for j in range(1, ITERS):
        solution = solution + coeffs[j][:, None] * krylov[j]
    return solution


def solution(mesh):
    return jax.shard_map(
        on_device,
        mesh=mesh,
        in_specs=(
            P("grp", "sub"),
            P("sub", None),
            P("sub"),
            P("sub", None),
            P("sub"),
            P("sub", None),
            P("sub", None),
            P("sub", None),
            P("sub", None),
            P(None, "sub"),
            P(("sub", "grp"), None),
        ),
        out_specs=P("grp", "sub"),
        check_vma=False,
    )
```

profile of v0, /device:TPU:0, one launch (start us, length us, event | category | flops | bytes accessed | tf_op | source)
XLA Modules:
  0.0 463.0 jit_solution(12258683345657579884)
XLA Ops:
  1.5 6.2 %all_gather.24 = bf16[64,512]{1,0:T(8,128)(2,1)S(1)} all-gather(bf16[64,128]{1,0:T(8,128)(2,1)S(1)} %convolution_convert_fusion.7), channel_id=1, replica_groups=mesh['sub'=8,'grp'=4] {'grp'}, dimensions={1}, use_global_device_ids=true | all-gather | bytes 81920 | tf_op jit(solution)/shard_map/all_gather | solution.py:54
  7.7 32.6 %all_gather.25 = bf16[512,512]{1,0:T(8,128)(2,1)S(1)} all-gather(bf16[64,512]{1,0:T(8,128)(2,1)S(1)} %all_gather.24), channel_id=1, replica_groups=mesh['sub'=8,'grp'=4] {'sub'}, dimensions={0}, use_global_device_ids=true | all-gather | bytes 589824 | tf_op jit(solution)/shard_map/all_gather | solution.py:57
  41.7 3.2 all-to-all-start
  53.7 21.2 %psum.70 = f32[128]{0:T(128)S(1)} all-reduce(f32[128]{0:T(128)S(1)} %get-tuple-element.18), channel_id=1, replica_groups=mesh['sub'=8,'grp'=4] {'sub'}, use_global_device_ids=true, to_apply=%region_1.0 | all-reduce | flops 128 | bytes 1024 | tf_op jit(solution)/shard_map/psum | solution.py:69
  77.0 4.7 %collective-permute-start = (bf16[128,128]{0,1:T(8,128)(2,1)S(1)}, bf16[128,128]{0,1:T(8,128)(2,1)S(1)}, u32[]{:S(2)}, u32[]{:S(2)}) collective-permute-start(bf16[128,128]{0,1:T(8,128)(2,1)S(1)} %select_bitcast_fusion.5), channel_id=1, source_target_pairs={{4,0},{8,4},{12,8},{16,12},{20,16},{24,20},{28,24},{0,28},{5,1},{9... | collective-permute-start | bytes 98312 | tf_op jit(solution)/shard_map/ppermute | solution.py:19
  91.2 5.3 %all_gather.26 = bf16[64,512]{1,0:T(8,128)(2,1)S(1)} all-gather(bf16[64,128]{1,0:T(8,128)(2,1)S(1)} %fusion.1), channel_id=1, replica_groups=mesh['sub'=8,'grp'=4] {'grp'}, dimensions={1}, use_global_device_ids=true | all-gather | bytes 81920 | tf_op jit(solution)/shard_map/all_gather | solution.py:54
  96.4 31.3 %all_gather.27 = bf16[512,512]{1,0:T(8,128)(2,1)S(1)} all-gather(bf16[64,512]{1,0:T(8,128)(2,1)S(1)} %all_gather.26), channel_id=1, replica_groups=mesh['sub'=8,'grp'=4] {'sub'}, dimensions={0}, use_global_device_ids=true | all-gather | bytes 589824 | tf_op jit(solution)/shard_map/all_gather | solution.py:57
  128.5 3.2 all-to-all-start.1
  137.0 19.2 %psum.71 = f32[128]{0:T(128)S(1)} all-reduce(f32[128]{0:T(128)S(1)} %get-tuple-element.20), channel_id=1, replica_groups=mesh['sub'=8,'grp'=4] {'sub'}, use_global_device_ids=true, to_apply=%region_5.7 | all-reduce | flops 128 | bytes 1024 | tf_op jit(solution)/shard_map/psum | solution.py:138
  156.4 17.1 %psum.72 = f32[128]{0:T(128)S(1)} all-reduce(f32[128]{0:T(128)S(1)} %multiply_reduce_fusion.7), channel_id=1, replica_groups=mesh['sub'=8,'grp'=4] {'sub'}, use_global_device_ids=true, to_apply=%region_7.9 | all-reduce | flops 128 | bytes 1024 | tf_op jit(solution)/shard_map/psum | solution.py:69
  202.1 5.3 %all_gather.28 = bf16[64,512]{1,0:T(8,128)(2,1)S(1)} all-gather(bf16[64,128]{1,0:T(8,128)(2,1)S(1)} %fusion.3), channel_id=1, replica_groups=mesh['sub'=8,'grp'=4] {'grp'}, dimensions={1}, use_global_device_ids=true | all-gather | bytes 81920 | tf_op jit(solution)/shard_map/all_gather | solution.py:54
  207.3 31.5 %all_gather.29 = bf16[512,512]{1,0:T(8,128)(2,1)S(1)} all-gather(bf16[64,512]{1,0:T(8,128)(2,1)S(1)} %all_gather.28), channel_id=1, replica_groups=mesh['sub'=8,'grp'=4] {'sub'}, dimensions={0}, use_global_device_ids=true | all-gather | bytes 589824 | tf_op jit(solution)/shard_map/all_gather | solution.py:57
  248.8 18.0 %psum.73 = f32[128]{0:T(128)S(1)} all-reduce(f32[128]{0:T(128)S(1)} %get-tuple-element.22), channel_id=1, replica_groups=mesh['sub'=8,'grp'=4] {'sub'}, use_global_device_ids=true, to_apply=%region_11.13 | all-reduce | flops 128 | bytes 1024 | tf_op jit(solution)/shard_map/psum | solution.py:138
  268.1 18.3 %psum.74 = f32[128]{0:T(128)S(1)} all-reduce(f32[128]{0:T(128)S(1)} %multiply_reduce_fusion.5), channel_id=1, replica_groups=mesh['sub'=8,'grp'=4] {'sub'}, use_global_device_ids=true, to_apply=%region_13.15 | all-reduce | flops 128 | bytes 1024 | tf_op jit(solution)/shard_map/psum | solution.py:138
  288.4 18.2 %psum.75 = f32[128]{0:T(128)S(1)} all-reduce(f32[128]{0:T(128)S(1)} %get-tuple-element.14), channel_id=1, replica_groups=mesh['sub'=8,'grp'=4] {'sub'}, use_global_device_ids=true, to_apply=%region_15.17 | all-reduce | flops 128 | bytes 1024 | tf_op jit(solution)/shard_map/psum | solution.py:69
  313.0 3.5 convolution_add_fusion.5
  317.9 3.6 collective-permute-start.4
  334.5 5.3 %all_gather.30 = bf16[64,512]{1,0:T(8,128)(2,1)S(1)} all-gather(bf16[64,128]{1,0:T(8,128)(2,1)S(1)} %fusion.5), channel_id=1, replica_groups=mesh['sub'=8,'grp'=4] {'grp'}, dimensions={1}, use_global_device_ids=true | all-gather | bytes 81920 | tf_op jit(solution)/shard_map/all_gather | solution.py:54
  339.7 31.5 %all_gather.31 = bf16[512,512]{1,0:T(8,128)(2,1)S(1)} all-gather(bf16[64,512]{1,0:T(8,128)(2,1)S(1)} %all_gather.30), channel_id=1, replica_groups=mesh['sub'=8,'grp'=4] {'sub'}, dimensions={0}, use_global_device_ids=true | all-gather | bytes 589824 | tf_op jit(solution)/shard_map/all_gather | solution.py:57
  372.0 3.2 all-to-all-start.3
  381.1 21.2 %psum.76 = f32[128]{0:T(128)S(1)} all-reduce(f32[128]{0:T(128)S(1)} %get-tuple-element.24), channel_id=1, replica_groups=mesh['sub'=8,'grp'=4] {'sub'}, use_global_device_ids=true, to_apply=%region_19.21 | all-reduce | flops 128 | bytes 1024 | tf_op jit(solution)/shard_map/psum | solution.py:138
  403.7 17.1 %psum.77 = f32[128]{0:T(128)S(1)} all-reduce(f32[128]{0:T(128)S(1)} %multiply_reduce_fusion.2), channel_id=1, replica_groups=mesh['sub'=8,'grp'=4] {'sub'}, use_global_device_ids=true, to_apply=%region_21.23 | all-reduce | flops 128 | bytes 1024 | tf_op jit(solution)/shard_map/psum | solution.py:138
  423.1 19.1 %psum.78 = f32[128]{0:T(128)S(1)} all-reduce(f32[128]{0:T(128)S(1)} %get-tuple-element.12), channel_id=1, replica_groups=mesh['sub'=8,'grp'=4] {'sub'}, use_global_device_ids=true, to_apply=%region_23.25 | all-reduce | flops 128 | bytes 1024 | tf_op jit(solution)/shard_map/psum | solution.py:138
  443.6 17.2 %psum.79 = f32[128]{0:T(128)S(1)} all-reduce(f32[128]{0:T(128)S(1)} %multiply_reduce_fusion), channel_id=1, replica_groups=mesh['sub'=8,'grp'=4] {'sub'}, use_global_device_ids=true, to_apply=%region_25.27 | all-reduce | flops 128 | bytes 1024 | tf_op jit(solution)/shard_map/psum | solution.py:69
  (181 shorter events, 105.4 us)
Async XLA Ops:
  0.0 50.0 %copy-start = (bf16[1024,1024]{1,0:T(8,128)(2,1)S(1)}, bf16[1024,1024]{1,0:T(8,128)(2,1)}, u32[]{:S(2)}) copy-start(bf16[1024,1024]{1,0:T(8,128)(2,1)} %param.16) | copy-start | bytes 6291460
  0.0 50.0 %copy-start.2 = (f32[128,1024]{1,0:T(8,128)S(1)}, f32[128,1024]{1,0:T(8,128)}, u32[]{:S(2)}) copy-start(f32[128,1024]{1,0:T(8,128)} %param.13) | copy-start | bytes 1572868
  7.7 44.7 %copy-start.1 = (bf16[64,1024]{1,0:T(8,128)(2,1)S(1)}, bf16[64,1024]{1,0:T(8,128)(2,1)}, u32[]{:S(2)}) copy-start(bf16[64,1024]{1,0:T(8,128)(2,1)} %param.22) | copy-start | bytes 393220
  41.7 10.6 %all-to-all-start = ((bf16[16,4,128]{2,0,1:T(8,128)(2,1)}), bf16[16,4,128]{2,0,1:T(8,128)(2,1)S(1)}, u32[]{:S(2)}, u32[]{:S(2)}) async-start(bf16[16,4,128]{2,0,1:T(8,128)(2,1)} %bitcast.121), calls=%async_computation | async-start | bytes 32768 | tf_op jit(solution)/shard_map/all_to_all | solution.py:60
  76.8 9.4 %collective-permute-start.1 = (bf16[128,128]{0,1:T(8,128)(2,1)S(1)}, bf16[128,128]{0,1:T(8,128)(2,1)S(1)}, u32[]{:S(2)}, u32[]{:S(2)}) collective-permute-start(bf16[128,128]{0,1:T(8,128)(2,1)S(1)} %select_bitcast_fusion.4), channel_id=1, source_target_pairs={{0,4},{4,8},{8,12},{12,16},{16,20},{20,24},{24,28},{28,0},{1,5},{5... | collective-permute-start | bytes 98312 | tf_op jit(solution)/shard_map/ppermute | solution.py:16
  77.0 9.5 %collective-permute-start = (bf16[128,128]{0,1:T(8,128)(2,1)S(1)}, bf16[128,128]{0,1:T(8,128)(2,1)S(1)}, u32[]{:S(2)}, u32[]{:S(2)}) collective-permute-start(bf16[128,128]{0,1:T(8,128)(2,1)S(1)} %select_bitcast_fusion.5), channel_id=1, source_target_pairs={{4,0},{8,4},{12,8},{16,12},{20,16},{24,20},{28,24},{0,28},{5,1},{9... | collective-permute-start | bytes 98312 | tf_op jit(solution)/shard_map/ppermute | solution.py:19
  86.8 40.9 %copy-start.10 = (bf16[16,512]{1,0:T(8,128)(2,1)S(1)}, bf16[16,512]{1,0:T(8,128)(2,1)}, u32[]{:S(2)}) copy-start(bf16[16,512]{1,0:T(8,128)(2,1)} %param.23) | copy-start | bytes 49156
  88.4 43.4 %copy-start.13 = (f32[1024]{0:T(1024)S(1)}, f32[1024]{0:T(1024)}, u32[]{:S(2)}) copy-start(f32[1024]{0:T(1024)} %param.17) | copy-start | bytes 12292
  128.5 7.1 %all-to-all-start.1 = ((bf16[16,4,128]{2,0,1:T(8,128)(2,1)}), bf16[16,4,128]{2,0,1:T(8,128)(2,1)S(1)}, u32[]{:S(2)}, u32[]{:S(2)}) async-start(bf16[16,4,128]{2,0,1:T(8,128)(2,1)} %bitcast.120), calls=%async_computation.1 | async-start | bytes 32768 | tf_op jit(solution)/shard_map/all_to_all | solution.py:60
  137.0 36.6 %copy-start.3 = (f32[128,1024]{1,0:T(8,128)}, f32[128,1024]{1,0:T(8,128)S(1)}, u32[]{:S(2)}) copy-start(f32[128,1024]{1,0:T(8,128)S(1)} %get-tuple-element.21) | copy-start | bytes 1572868
  181.2 10.0 %collective-permute-start.3 = (bf16[128,128]{0,1:T(8,128)(2,1)S(1)}, bf16[128,128]{0,1:T(8,128)(2,1)S(1)}, u32[]{:S(2)}, u32[]{:S(2)}) collective-permute-start(bf16[128,128]{0,1:T(8,128)(2,1)S(1)} %select_bitcast_fusion.2), channel_id=1, source_target_pairs={{0,4},{4,8},{8,12},{12,16},{16,20},{20,24},{24,28},{28,0},{1,5},{5... | collective-permute-start | bytes 98312 | tf_op jit(solution)/shard_map/ppermute | solution.py:16
  183.3 8.3 %collective-permute-start.2 = (bf16[128,128]{0,1:T(8,128)(2,1)S(1)}, bf16[128,128]{0,1:T(8,128)(2,1)}, u32[]{:S(2)}, u32[]{:S(2)}) collective-permute-start(bf16[128,128]{0,1:T(8,128)(2,1)S(1)} %select_bitcast_fusion.3), channel_id=1, source_target_pairs={{4,0},{8,4},{12,8},{16,12},{20,16},{24,20},{28,24},{0,28},{5,1},{9... | collective-permute-start | bytes 98312 | tf_op jit(solution)/shard_map/ppermute | solution.py:19
  195.7 47.2 %copy-start.14 = (f32[1024]{0:T(1024)S(1)}, f32[1024]{0:T(1024)}, u32[]{:S(2)}) copy-start(f32[1024]{0:T(1024)} %param.17) | copy-start | bytes 12292
  239.7 7.1 %all-to-all-start.2 = ((bf16[16,4,128]{2,0,1:T(8,128)(2,1)}), bf16[16,4,128]{2,0,1:T(8,128)(2,1)S(1)}, u32[]{:S(2)}, u32[]{:S(2)}) async-start(bf16[16,4,128]{2,0,1:T(8,128)(2,1)} %bitcast.119), calls=%async_computation.2 | async-start | bytes 32768 | tf_op jit(solution)/shard_map/all_to_all | solution.py:60
  266.8 39.8 %copy-start.26 = (f32[128]{0:T(128)}, f32[128]{0:T(128)S(1)}, u32[]{:S(2)}) copy-start(f32[128]{0:T(128)S(1)} %psum.73) | copy-start | bytes 1540
  316.6 7.0 %collective-permute-start.5 = (bf16[128,128]{0,1:T(8,128)(2,1)S(1)}, bf16[128,128]{0,1:T(8,128)(2,1)S(1)}, u32[]{:S(2)}, u32[]{:S(2)}) collective-permute-start(bf16[128,128]{0,1:T(8,128)(2,1)S(1)} %select_bitcast_fusion), channel_id=1, source_target_pairs={{0,4},{4,8},{8,12},{12,16},{16,20},{20,24},{24,28},{28,0},{1,5},{5... | collective-permute-start | bytes 98312 | tf_op jit(solution)/shard_map/ppermute | solution.py:16
  317.9 6.0 %collective-permute-start.4 = (bf16[128,128]{0,1:T(8,128)(2,1)S(1)}, bf16[128,128]{0,1:T(8,128)(2,1)}, u32[]{:S(2)}, u32[]{:S(2)}) collective-permute-start(bf16[128,128]{0,1:T(8,128)(2,1)S(1)} %select_bitcast_fusion.1), channel_id=1, source_target_pairs={{4,0},{8,4},{12,8},{16,12},{20,16},{24,20},{28,24},{0,28},{5,1},{9... | collective-permute-start | bytes 98312 | tf_op jit(solution)/shard_map/ppermute | solution.py:19
  328.1 47.1 %copy-start.15 = (f32[1024]{0:T(1024)S(1)}, f32[1024]{0:T(1024)}, u32[]{:S(2)}) copy-start(f32[1024]{0:T(1024)} %param.17) | copy-start | bytes 12292
  372.0 7.1 %all-to-all-start.3 = ((bf16[16,4,128]{2,0,1:T(8,128)(2,1)}), bf16[16,4,128]{2,0,1:T(8,128)(2,1)S(1)}, u32[]{:S(2)}, u32[]{:S(2)}) async-start(bf16[16,4,128]{2,0,1:T(8,128)(2,1)} %bitcast.118), calls=%async_computation.3 | async-start | bytes 32768 | tf_op jit(solution)/shard_map/all_to_all | solution.py:60
  378.0 42.8 %copy-start.23 = (f32[128]{0:T(128)S(1)}, f32[128]{0:T(128)}, u32[]{:S(2)}) copy-start(f32[128]{0:T(128)} %copy-done.22) | copy-start | bytes 1540
  403.6 57.2 %copy-start.27 = (f32[128]{0:T(128)S(1)}, f32[128]{0:T(128)}, u32[]{:S(2)}) copy-start(f32[128]{0:T(128)} %copy-done.26) | copy-start | bytes 1540
  403.7 57.2 %copy-start.34 = (f32[128]{0:T(128)S(1)}, f32[128]{0:T(128)}, u32[]{:S(2)}) copy-start(f32[128]{0:T(128)} %copy-done.33) | copy-start | bytes 1540
  403.7 57.2 %copy-start.38 = (f32[128]{0:T(128)S(1)}, f32[128]{0:T(128)}, u32[]{:S(2)}) copy-start(f32[128]{0:T(128)} %copy-done.37) | copy-start | bytes 1540
  403.7 57.2 %copy-start.40 = (f32[128]{0:T(128)S(1)}, f32[128]{0:T(128)}, u32[]{:S(2)}) copy-start(f32[128]{0:T(128)} %copy-done.39) | copy-start | bytes 1540
  (27 other events, 327.7 us)
where the time goes:
time: 465 us; the launch traced here: 463 us
  blocking collectives  335 us (72%)
  other arithmetic  37.1 us (8%)
  matrix products  35.6 us (8%)
  starting transfers between devices  27.4 us (6%)
  local copies, waits for them, and re-layouts  23.7 us (5%)
    all_gather x4, blocking collectives, apply_solve(): lax.all_gather(widened, 'sub', axis=0, tiled=True)  127 us
    psum x6, blocking collectives, on_device(): height_i = lax.psum(jnp.sum(candidate * krylov[i], axis=1), 'sub')  113 us
    psum x4, blocking collectives, norm_of(): return jnp.sqrt(lax.psum(squares, 'sub') + EPS)  73.7 us
    dot_general x11, matrix products, contract_last(): lax.dot_general(left, right, (((1,), (1,)), ((), ())), preferred_element_...  24.7 us
    all_gather x4, blocking collectives, apply_solve(): widened = lax.all_gather(partial_res, 'grp', axis=1, tiled=True)  21.9 us
    all_to_all x4, starting transfers between devices, apply_solve(): lax.all_to_all(solved_part, 'grp', split_axis=1, concat_axis=0, tiled=True)  13 us
    ppermute x3, starting transfers between devices, extended(): lax.ppermute(lax.slice_in_dim(block, 0, width, axis=dim), axis, backward)  11.1 us
  transfers between devices with their start and end apart: 10, of which 3 were waited for; matrix products, arithmetic and copies ran while one was open for 6% of the time, Pallas kernels for 0%

commit v1 on v0

--- a/solution.py
+++ b/solution.py
@@ -51,7 +51,12 @@
     vector_b = vector.astype(jnp.bfloat16)
     local_term = contract_last(vector_b, solve_block)
     partial_res = contract_last(coarse_basis, vector_b).astype(jnp.bfloat16)
-    widened = lax.all_gather(partial_res, "grp", axis=1, tiled=True)
+    ring = [partial_res]
+    for hop in range(3):
+        ring.append(lax.ppermute(ring[-1], "grp", [(dev, (dev + 1) % 4) for dev in range(4)]))
+    widened = jnp.roll(
+        jnp.concatenate(ring[::-1], axis=1), (lax.axis_index("grp") + 1) * ring[0].shape[1], axis=1
+    )
     solved_part = jnp.dot(
         coarse_inverse,
         lax.all_gather(widened, "sub", axis=0, tiled=True),

time: 465 us -> 473 us (1.017)
  waiting for transfers between devices: 3.16 us -> 34 us
  blocking collectives: 335 us -> 314 us
    ppermute x0 -> x12, waiting for transfers between devices: none -> 27.1 us  [apply_solve(): lax.ppermute(ring[-1], 'grp', [(dev, (dev + 1) % 4) for dev in range(4)])]
    all_gather x4 -> x0, blocking collectives: 21.9 us -> none  [apply_solve(): widened = lax.all_gather(partial_res, 'grp', axis=1, tiled=True)]
  transfers between devices with their start and end apart: 10 -> 22, of which waited for: 3 -> 16; matrix products, arithmetic and copies ran while one was open for 6% -> 6% of each run, Pallas kernels for 0% -> 0%
where the time goes in v1:
time: 473 us; the launch traced here: 471 us
  blocking collectives  314 us (66%)
  matrix products  34.5 us (7%)
  waiting for transfers between devices  34 us (7%)
  other arithmetic  33.7 us (7%)
  starting transfers between devices  30.5 us (6%)
  local copies, waits for them, and re-layouts  23.7 us (5%)
    all_gather x4, blocking collectives, apply_solve(): lax.all_gather(widened, 'sub', axis=0, tiled=True)  127 us
    psum x6, blocking collectives, on_device(): height_i = lax.psum(jnp.sum(candidate * krylov[i], axis=1), 'sub')  113 us
    psum x4, blocking collectives, norm_of(): return jnp.sqrt(lax.psum(squares, 'sub') + EPS)  73.7 us
    ppermute x12, waiting for transfers between devices, apply_solve(): lax.ppermute(ring[-1], 'grp', [(dev, (dev + 1) % 4) for dev in range(4)])  27.1 us
    dot_general x11, matrix products, contract_last(): lax.dot_general(left, right, (((1,), (1,)), ((), ())), preferred_element_...  24.5 us
    all_to_all x4, starting transfers between devices, apply_solve(): lax.all_to_all(solved_part, 'grp', split_axis=1, concat_axis=0, tiled=True)  13 us
    ppermute x3, starting transfers between devices, extended(): lax.ppermute(lax.slice_in_dim(block, 0, width, axis=dim), axis, backward)  11.2 us
  transfers between devices with their start and end apart: 22, of which 16 were waited for; matrix products, arithmetic and copies ran while one was open for 6% of the time, Pallas kernels for 0%

profile of v1, /device:TPU:0, one launch (start us, length us, event | category | flops | bytes accessed | tf_op | source)
XLA Modules:
  0.0 471.2 jit_solution(17508191079691785960)
XLA Ops:
  11.8 32.6 %all_gather.12 = bf16[512,512]{1,0:T(8,128)(2,1)S(1)} all-gather(bf16[64,512]{1,0:T(8,128)(2,1)S(1)} %fusion.39), channel_id=1, replica_groups=mesh['sub'=8,'grp'=4] {'sub'}, dimensions={0}, use_global_device_ids=true | all-gather | bytes 589824 | tf_op jit(solution)/shard_map/all_gather | solution.py:62
  45.2 3.3 all-to-all-start
  48.5 3.8 all-to-all-done
  52.6 21.2 %psum.70 = f32[128]{0:T(128)S(1)} all-reduce(f32[128]{0:T(128)S(1)} %get-tuple-element.19), channel_id=1, replica_groups=mesh['sub'=8,'grp'=4] {'sub'}, use_global_device_ids=true, to_apply=%region_1.3 | all-reduce | flops 128 | bytes 1024 | tf_op jit(solution)/shard_map/psum | solution.py:74
  75.8 4.8 %collective-permute-start.3 = (bf16[128,128]{0,1:T(8,128)(2,1)S(1)}, bf16[128,128]{0,1:T(8,128)(2,1)}, u32[]{:S(2)}, u32[]{:S(2)}) collective-permute-start(bf16[128,128]{0,1:T(8,128)(2,1)S(1)} %select_bitcast_fusion.5), channel_id=1, source_target_pairs={{4,0},{8,4},{12,8},{16,12},{20,16},{24,20},{28,24},{0,28},{5,1},{9... | collective-permute-start | bytes 98312 | tf_op jit(solution)/shard_map/ppermute | solution.py:19
  80.5 3.2 convolution_add_fusion.9
  99.4 31.3 %all_gather.13 = bf16[512,512]{1,0:T(8,128)(2,1)S(1)} all-gather(bf16[64,512]{1,0:T(8,128)(2,1)S(1)} %fusion.32), channel_id=1, replica_groups=mesh['sub'=8,'grp'=4] {'sub'}, dimensions={0}, use_global_device_ids=true | all-gather | bytes 589824 | tf_op jit(solution)/shard_map/all_gather | solution.py:62
  131.5 3.2 all-to-all-start.1
  139.9 19.4 %psum.71 = f32[128]{0:T(128)S(1)} all-reduce(f32[128]{0:T(128)S(1)} %get-tuple-element.21), channel_id=1, replica_groups=mesh['sub'=8,'grp'=4] {'sub'}, use_global_device_ids=true, to_apply=%region_5.8 | all-reduce | flops 128 | bytes 1024 | tf_op jit(solution)/shard_map/psum | solution.py:143
  159.6 17.1 %psum.72 = f32[128]{0:T(128)S(1)} all-reduce(f32[128]{0:T(128)S(1)} %multiply_reduce_fusion.7), channel_id=1, replica_groups=mesh['sub'=8,'grp'=4] {'sub'}, use_global_device_ids=true, to_apply=%region_7.10 | all-reduce | flops 128 | bytes 1024 | tf_op jit(solution)/shard_map/psum | solution.py:74
  189.1 3.2 convolution_add_fusion.7
  212.8 31.7 %all_gather.14 = bf16[512,512]{1,0:T(8,128)(2,1)S(1)} all-gather(bf16[64,512]{1,0:T(8,128)(2,1)S(1)} %fusion.25), channel_id=1, replica_groups=mesh['sub'=8,'grp'=4] {'sub'}, dimensions={0}, use_global_device_ids=true | all-gather | bytes 589824 | tf_op jit(solution)/shard_map/all_gather | solution.py:62
  245.3 3.2 all-to-all-start.2
  254.4 18.0 %psum.73 = f32[128]{0:T(128)S(1)} all-reduce(f32[128]{0:T(128)S(1)} %get-tuple-element.23), channel_id=1, replica_groups=mesh['sub'=8,'grp'=4] {'sub'}, use_global_device_ids=true, to_apply=%region_11.14 | all-reduce | flops 128 | bytes 1024 | tf_op jit(solution)/shard_map/psum | solution.py:143
  273.7 18.2 %psum.74 = f32[128]{0:T(128)S(1)} all-reduce(f32[128]{0:T(128)S(1)} %multiply_reduce_fusion.5), channel_id=1, replica_groups=mesh['sub'=8,'grp'=4] {'sub'}, use_global_device_ids=true, to_apply=%region_13.16 | all-reduce | flops 128 | bytes 1024 | tf_op jit(solution)/shard_map/psum | solution.py:143
  294.0 18.2 %psum.75 = f32[128]{0:T(128)S(1)} all-reduce(f32[128]{0:T(128)S(1)} %get-tuple-element.15), channel_id=1, replica_groups=mesh['sub'=8,'grp'=4] {'sub'}, use_global_device_ids=true, to_apply=%region_15.18 | all-reduce | flops 128 | bytes 1024 | tf_op jit(solution)/shard_map/psum | solution.py:74
  318.7 3.5 convolution_add_fusion.5
  323.5 3.7 collective-permute-start.13
  347.7 31.4 %all_gather.15 = bf16[512,512]{1,0:T(8,128)(2,1)S(1)} all-gather(bf16[64,512]{1,0:T(8,128)(2,1)S(1)} %fusion.18), channel_id=1, replica_groups=mesh['sub'=8,'grp'=4] {'sub'}, dimensions={0}, use_global_device_ids=true | all-gather | bytes 589824 | tf_op jit(solution)/shard_map/all_gather | solution.py:62
  380.0 3.2 all-to-all-start.3
  389.1 21.4 %psum.76 = f32[128]{0:T(128)S(1)} all-reduce(f32[128]{0:T(128)S(1)} %get-tuple-element.25), channel_id=1, replica_groups=mesh['sub'=8,'grp'=4] {'sub'}, use_global_device_ids=true, to_apply=%region_19.22 | all-reduce | flops 128 | bytes 1024 | tf_op jit(solution)/shard_map/psum | solution.py:143
  411.9 17.1 %psum.77 = f32[128]{0:T(128)S(1)} all-reduce(f32[128]{0:T(128)S(1)} %multiply_reduce_fusion.2), channel_id=1, replica_groups=mesh['sub'=8,'grp'=4] {'sub'}, use_global_device_ids=true, to_apply=%region_21.24 | all-reduce | flops 128 | bytes 1024 | tf_op jit(solution)/shard_map/psum | solution.py:143
  431.3 19.1 %psum.78 = f32[128]{0:T(128)S(1)} all-reduce(f32[128]{0:T(128)S(1)} %get-tuple-element.13), channel_id=1, replica_groups=mesh['sub'=8,'grp'=4] {'sub'}, use_global_device_ids=true, to_apply=%region_23.26 | all-reduce | flops 128 | bytes 1024 | tf_op jit(solution)/shard_map/psum | solution.py:143
  451.8 17.2 %psum.79 = f32[128]{0:T(128)S(1)} all-reduce(f32[128]{0:T(128)S(1)} %multiply_reduce_fusion), channel_id=1, replica_groups=mesh['sub'=8,'grp'=4] {'sub'}, use_global_device_ids=true, to_apply=%region_25.28 | all-reduce | flops 128 | bytes 1024 | tf_op jit(solution)/shard_map/psum | solution.py:74
  (204 shorter events, 121.2 us)
Async XLA Ops:
  1.5 3.9 collective-permute-start
  2.7 72.8 %copy-start.21 = (pred[128]{0:T(512)(128)(4,1)}, pred[128]{0:T(512)(128)(4,1)S(1)}, u32[]{:S(2)}) copy-start(pred[128]{0:T(512)(128)(4,1)S(1)} %get-tuple-element.29) | copy-start | bytes 388
  2.7 73.0 %copy-start.19 = (pred[128]{0:T(512)(128)(4,1)}, pred[128]{0:T(512)(128)(4,1)S(1)}, u32[]{:S(2)}) copy-start(pred[128]{0:T(512)(128)(4,1)S(1)} %get-tuple-element.30) | copy-start | bytes 388
  5.3 3.2 collective-permute-start.1
  8.5 3.2 collective-permute-start.2
  45.2 7.1 %all-to-all-start = ((bf16[16,4,128]{2,0,1:T(8,128)(2,1)}), bf16[16,4,128]{2,0,1:T(8,128)(2,1)S(1)}, u32[]{:S(2)}, u32[]{:S(2)}) async-start(bf16[16,4,128]{2,0,1:T(8,128)(2,1)} %bitcast.121), calls=%async_computation | async-start | bytes 32768 | tf_op jit(solution)/shard_map/all_to_all | solution.py:65
  75.6 9.4 %collective-permute-start.4 = (bf16[128,128]{0,1:T(8,128)(2,1)S(1)}, bf16[128,128]{0,1:T(8,128)(2,1)S(1)}, u32[]{:S(2)}, u32[]{:S(2)}) collective-permute-start(bf16[128,128]{0,1:T(8,128)(2,1)S(1)} %select_bitcast_fusion.4), channel_id=1, source_target_pairs={{0,4},{4,8},{8,12},{12,16},{16,20},{20,24},{24,28},{28,0},{1,5},{5... | collective-permute-start | bytes 98312 | tf_op jit(solution)/shard_map/ppermute | solution.py:16
  75.8 9.5 %collective-permute-start.3 = (bf16[128,128]{0,1:T(8,128)(2,1)S(1)}, bf16[128,128]{0,1:T(8,128)(2,1)}, u32[]{:S(2)}, u32[]{:S(2)}) collective-permute-start(bf16[128,128]{0,1:T(8,128)(2,1)S(1)} %select_bitcast_fusion.5), channel_id=1, source_target_pairs={{4,0},{8,4},{12,8},{16,12},{20,16},{24,20},{28,24},{0,28},{5,1},{9... | collective-permute-start | bytes 98312 | tf_op jit(solution)/shard_map/ppermute | solution.py:19
  89.8 3.2 collective-permute-start.5
  93.0 3.2 collective-permute-start.6
  96.1 3.2 collective-permute-start.7
  131.5 7.1 %all-to-all-start.1 = ((bf16[16,4,128]{2,0,1:T(8,128)(2,1)}), bf16[16,4,128]{2,0,1:T(8,128)(2,1)S(1)}, u32[]{:S(2)}, u32[]{:S(2)}) async-start(bf16[16,4,128]{2,0,1:T(8,128)(2,1)} %bitcast.120), calls=%async_computation.1 | async-start | bytes 32768 | tf_op jit(solution)/shard_map/all_to_all | solution.py:65
  184.3 10.0 %collective-permute-start.9 = (bf16[128,128]{0,1:T(8,128)(2,1)S(1)}, bf16[128,128]{0,1:T(8,128)(2,1)S(1)}, u32[]{:S(2)}, u32[]{:S(2)}) collective-permute-start(bf16[128,128]{0,1:T(8,128)(2,1)S(1)} %select_bitcast_fusion.2), channel_id=1, source_target_pairs={{0,4},{4,8},{8,12},{12,16},{16,20},{20,24},{24,28},{28,0},{1,5},{5... | collective-permute-start | bytes 98312 | tf_op jit(solution)/shard_map/ppermute | solution.py:16
  186.4 8.3 %collective-permute-start.8 = (bf16[128,128]{0,1:T(8,128)(2,1)S(1)}, bf16[128,128]{0,1:T(8,128)(2,1)}, u32[]{:S(2)}, u32[]{:S(2)}) collective-permute-start(bf16[128,128]{0,1:T(8,128)(2,1)S(1)} %select_bitcast_fusion.3), channel_id=1, source_target_pairs={{4,0},{8,4},{12,8},{16,12},{20,16},{24,20},{28,24},{0,28},{5,1},{9... | collective-permute-start | bytes 98312 | tf_op jit(solution)/shard_map/ppermute | solution.py:19
  203.1 3.2 collective-permute-start.10
  206.3 3.2 collective-permute-start.11
  209.5 3.2 collective-permute-start.12
  245.3 7.1 %all-to-all-start.2 = ((bf16[16,4,128]{2,0,1:T(8,128)(2,1)}), bf16[16,4,128]{2,0,1:T(8,128)(2,1)S(1)}, u32[]{:S(2)}, u32[]{:S(2)}) async-start(bf16[16,4,128]{2,0,1:T(8,128)(2,1)} %bitcast.119), calls=%async_computation.2 | async-start | bytes 32768 | tf_op jit(solution)/shard_map/all_to_all | solution.py:65
  322.3 7.0 %collective-permute-start.14 = (bf16[128,128]{0,1:T(8,128)(2,1)S(1)}, bf16[128,128]{0,1:T(8,128)(2,1)S(1)}, u32[]{:S(2)}, u32[]{:S(2)}) collective-permute-start(bf16[128,128]{0,1:T(8,128)(2,1)S(1)} %select_bitcast_fusion), channel_id=1, source_target_pairs={{0,4},{4,8},{8,12},{12,16},{16,20},{20,24},{24,28},{28,0},{1,5},{5... | collective-permute-start | bytes 98312 | tf_op jit(solution)/shard_map/ppermute | solution.py:16
  323.5 6.0 %collective-permute-start.13 = (bf16[128,128]{0,1:T(8,128)(2,1)S(1)}, bf16[128,128]{0,1:T(8,128)(2,1)}, u32[]{:S(2)}, u32[]{:S(2)}) collective-permute-start(bf16[128,128]{0,1:T(8,128)(2,1)S(1)} %select_bitcast_fusion.1), channel_id=1, source_target_pairs={{4,0},{8,4},{12,8},{16,12},{20,16},{24,20},{28,24},{0,28},{5,1},{9... | collective-permute-start | bytes 98312 | tf_op jit(solution)/shard_map/ppermute | solution.py:19
  338.1 3.2 collective-permute-start.15
  341.3 3.2 collective-permute-start.16
  344.5 3.2 collective-permute-start.17
  380.0 7.1 %all-to-all-start.3 = ((bf16[16,4,128]{2,0,1:T(8,128)(2,1)}), bf16[16,4,128]{2,0,1:T(8,128)(2,1)S(1)}, u32[]{:S(2)}, u32[]{:S(2)}) async-start(bf16[16,4,128]{2,0,1:T(8,128)(2,1)} %bitcast.118), calls=%async_computation.3 | async-start | bytes 32768 | tf_op jit(solution)/shard_map/all_to_all | solution.py:65
  (40 other events, 946.5 us)
